TPU v7x, 512 devices: a whole 4x4x16 slice. The times are simulated.
512 devices in a mesh: rows: 32 (over z_lo, x), cols: 16 (over y, z_hi, core).
Axes of the slice: x: 4, y: 4, z: 16 (z_hi: 2, z_lo: 8; z = z_hi * 8 + z_lo), core: 2. Of those that a mesh axis runs over, the one named last changes fastest.
Arguments:
- left_feat: bfloat16 [320, 32, 2048], P(None, 'rows', 'cols'), may hold values from -6 to 6
- right_feat: bfloat16 [320, 32, 2048], P(None, 'rows', 'cols'), may hold values from -6 to 6
- grad_out: bfloat16 [32, 48, 32, 2048], P(None, None, 'rows', 'cols'), may hold values from -6 to 6
- conv_weight: bfloat16 [32, 40, 3, 3, 3], replicated, may hold values from -0.21875 to 0.21875
Outputs:
- grad_left: bfloat16 [320, 32, 2048], P(None, 'rows', 'cols')
- grad_right: bfloat16 [320, 32, 2048], P(None, 'rows', 'cols')
- grad_weight: float32 [32, 40, 3, 3, 3], replicated
All inputs are finite; a program needn't handle non-finite values.
Results may differ from a plain program's by a relative error of at most 0.0029.
Values may be sent and summed in bfloat16 or wider, within the bound.
A program may use at most 64 MiB of HBM per device.

v0:
```python
import math
import jax
import jax.numpy as jnp
from jax import lax
from jax.sharding import PartitionSpec as P


def from_behind(shard, axis, by):
    count = lax.axis_size(axis)
    pairs = [(i, i + by) for i in range(count) if 0 <= i + by < count]
    return lax.ppermute(shard, axis, pairs)


def padded_2(shard, sides, width):
    for axis, dim in sides:
        count, length = (lax.axis_size(axis), shard.shape[dim])
        up = [(i, (i + 1) % count) for i in range(count - 1)]
        down = [(j, i) for i, j in up]
        last = lax.slice_in_dim(shard, length - width, length, axis=dim)
        initial = lax.slice_in_dim(shard, 0, width, axis=dim)
        before = lax.ppermute(last, axis, up)
        after = lax.ppermute(initial, axis, down)
        shard = jnp.concatenate([before, shard, after], axis=dim)
    return shard


def correlate(left_band, right_ext, levels, groups):
    channels, band_rows, tile_width = left_band.shape
    group_size = channels // groups
    left_wide = left_band.astype(jnp.float32)
    start_volume = jnp.zeros((groups, levels, band_rows, tile_width), jnp.float32)

    def correlate_one_level(level, volume):
        offset = (levels - 1 - level).astype(jnp.int32)
        shifted = lax.dynamic_slice_in_dim(right_ext, offset, tile_width, 2).astype(jnp.float32)
        product = (left_wide * shifted).reshape(groups, group_size, band_rows, tile_width)
        slab = jnp.sum(product, axis=1) * (1.0 / group_size)
        return lax.dynamic_update_slice_in_dim(volume, slab[:, None], level, 1)

    return lax.fori_loop(0, levels, correlate_one_level, start_volume)


def feature_grads(grad_volume, left_band, right_ext, levels, groups):
    channels, band_rows, tile_width = left_band.shape
    group_size = channels // groups
    left_wide = left_band.astype(jnp.float32).reshape(groups, group_size, band_rows, tile_width)
    start_left = jnp.zeros((groups, group_size, band_rows, tile_width), jnp.float32)
    start_ext = jnp.zeros((channels, band_rows, tile_width + levels - 1), jnp.float32)

    def feature_one_level(level, carry):
        grad_left, grad_ext = carry
        offset = (levels - 1 - level).astype(jnp.int32)
        shifted = lax.dynamic_slice_in_dim(right_ext, offset, tile_width, 2).astype(jnp.float32)
        slab = lax.dynamic_slice_in_dim(grad_volume, level, 1, 1)
        grad_left = grad_left + slab * shifted.reshape(groups, group_size, band_rows, tile_width)
        spread = (slab * left_wide).reshape(channels, band_rows, tile_width)
        current = lax.dynamic_slice_in_dim(grad_ext, offset, tile_width, 2)
        grad_ext = lax.dynamic_update_slice_in_dim(grad_ext, current + spread, offset, 2)
        return (grad_left, grad_ext)

    grad_left, grad_ext = lax.fori_loop(0, levels, feature_one_level, (start_left, start_ext))
    scale = 1.0 / group_size
    return (grad_left.reshape(channels, band_rows, tile_width) * scale, grad_ext * scale)


def kernel_terms(volume, padded, levels, band_rows, tile_width):
    terms = []
    for along_d in range(3):
        for along_h in range(3):
            for along_w in range(3):
                window_cut = padded[
                    :,
                    2 - along_d : 2 - along_d + levels,
                    2 - along_h : 2 - along_h + band_rows,
                    2 - along_w : 2 - along_w + tile_width,
                ]
                terms.append(
                    lax.dot_general(
                        window_cut,
                        volume,
                        (((1, 2, 3), (1, 2, 3)), ((), ())),
                        preferred_element_type=jnp.float32,
                    )
                )
    stacked = jnp.stack(terms, axis=-1)
    return stacked.reshape(stacked.shape[0], stacked.shape[1], 3, 3, 3)


def shards(left_feat, right_feat, grad_out, conv_weight):
    channels, band_rows, tile_width = left_feat.shape
    levels = grad_out.shape[1]
    groups = conv_weight.shape[1]
    margin_cols = levels - 1
    shifted_tile = from_behind(right_feat, "cols", 1)
    border = shifted_tile[:, :, tile_width - margin_cols :]
    right_ext = jnp.concatenate([border, right_feat], axis=2)
    volume = correlate(left_feat, right_ext, levels, groups).astype(jnp.bfloat16)
    padded = padded_2(grad_out, (("rows", 2), ("cols", 3)), 1)
    padded = jnp.pad(padded, ((0, 0), (1, 1), (0, 0), (0, 0)))
    flipped = jnp.transpose(jnp.flip(conv_weight, (2, 3, 4)), (1, 0, 2, 3, 4))
    layout = ("NCDHW", "OIDHW", "NCDHW")
    kernel_local = kernel_terms(volume, padded, levels, band_rows, tile_width)
    summed = lax.psum(kernel_local, ("rows", "cols"))
    grad_volume = lax.conv_general_dilated(
        padded[None],
        flipped,
        (1, 1, 1),
        "VALID",
        dimension_numbers=layout,
        preferred_element_type=jnp.float32,
    )[0]
    cells = levels * band_rows * lax.axis_size("rows") * tile_width * lax.axis_size("cols")
    grad_weight = summed * (1.0 / math.sqrt(cells))
    grad_left, grad_ext = feature_grads(grad_volume, left_feat, right_ext, levels, groups)
    own_part = grad_ext[:, :, margin_cols:]
    spill = grad_ext[:, :, :margin_cols]
    spill_tile = jnp.pad(spill, ((0, 0), (0, 0), (tile_width - margin_cols, 0)))
    arrived = from_behind(spill_tile, "cols", -1)
    grad_right = own_part + arrived
    return (grad_left.astype(jnp.bfloat16), grad_right.astype(jnp.bfloat16), grad_weight)


def solution(mesh):
    placed = (P(None, "rows", "cols"), P(None, "rows", "cols"), P(None, None, "rows", "cols"), P())
    return jax.shard_map(
        shards,
        mesh=mesh,
        in_specs=placed,
        out_specs=(P(None, "rows", "cols"), P(None, "rows", "cols"), P()),
        check_vma=False,
    )
```

profile of v0, /device:TPU:2, one launch (start us, length us, event | category | flops | bytes accessed | tf_op | source)
XLA Modules:
  0.0 600.7 jit_solution(4668678989046985764)
XLA Ops:
  8.4 3.4 collective-permute-start
  11.8 5.7 collective-permute-start.1
  21.1 46.2 %while.33 = (s32[]{:T(128)}, f32[40,48,1,128]{3,2,1,0:T(1,128)}, bf16[320,1,175]{2,0,1:T(8,128)(2,1)S(1)}, f32[320,1,128]{2,1,0:T(1,128)S(1)}, s32[]{:T(128)}, /*index=5*/s32[]{:T(128)}, s32[]{:T(128)}, s32[]{:T(128)}) while((s32[]{:T(128)}, f32[40,48,1,128]{3,2,1,0:T(1,128)}, bf16[320,1,175]{2,0,1:T(8,128)(2,1)S(1)}, ...), condition=%wide.region_4.5_spmd, body=%wide.region_2.4_spmd.sunk | while | flops 122886 | bytes 840327 | solution.py:40
  69.5 1.6 fusion.78
  71.1 2.5 copy.85
  73.6 15.5 %collective-permute-start.2 = (bf16[32,48,3,1]{1,0,3,2:T(8,128)(2,1)S(1)}, bf16[32,48,3,1]{1,0,3,2:T(8,128)(2,1)S(1)}, u32[]{:S(2)}, u32[]{:S(2)}) collective-permute-start(bf16[32,48,3,1]{1,0,3,2:T(8,128)(2,1)S(1)} %copy.85), channel_id=1, source_target_pairs={{0,1},{1,2},{2,3},{3,4},{4,5},{5,6},{6,7},{7,8},{8,9},{9,10},{10,1... | collective-permute-start | bytes 27656 | tf_op jit(solution)/shard_map/ppermute | solution.py:21
  93.1 1.9 copy.87
  95.0 9.2 %collective-permute-done.3 = bf16[32,48,3,1]{1,0,3,2:T(8,128)(2,1)S(1)} collective-permute-done((bf16[32,48,3,1]{1,0,3,2:T(8,128)(2,1)S(1)}, bf16[32,48,3,1]{1,0,3,2:T(8,128)(2,1)S(1)}, u32[]{:S(2)}, u32[]{:S(2)}) %collective-permute-start.3) | collective-permute-done | bytes 9248 | tf_op jit(solution)/shard_map/ppermute | solution.py:22
  104.2 2.9 copy.88
  107.1 2.8 fusion.16
  109.8 2.7 fusion.80
  122.9 5.7 copy.134
  128.6 4.3 pad.10.clone
  132.9 7.2 %copy.91 = bf16[32,50,3,1,8,17]{0,4,5,2,1,3:T(8,128)(2,1)} copy(bf16[32,50,3,1,8,17]{1,0,5,4,2,3:T(8,128)(2,1)} %bitcast.194) | data formatting | bytes 2611200 | tf_op jit(solution)/shard_map/conv_general_dilated | solution.py:104
  141.4 10.0 %fusion.17 = f32[48,1,8,17,40]{4,2,3,1,0:T(8,128)} fusion(bf16[32,40,3,3,3]{1,0,4,3,2:T(8,128)(2,1)S(1)} %copy-done, bf16[32,50,3,1,7,2]{0,4,5,2,1,3:T(8,128)(2,1)S(1)} %slice.141, bf16[32,50,3,1,8,17]{0,4,5,2,1,3:T(8,128)(2,1)} %copy.91, pred[8,17]{0,1:T(8,128)(4,1)S(1)} %copy-done.11), kind=kOutput, calls=%fused_computation.30 | convolution fusion | flops 455854080 | bytes 2553736 | tf_op jit(solution)/shard_map/conv_general_dilated | solution.py:104
  151.4 3.5 copy.92
  155.0 1.7 slice_bitcast_fusion
  156.7 2.5 copy.94
  159.2 109.2 %while.34 = (s32[]{:T(128)}, f32[40,8,1,128]{3,2,1,0:T(1,128)S(1)}, f32[320,1,175]{2,0,1:T(8,128)S(1)}, f32[40,48,1,128]{3,0,2,1:T(8,128)S(1)}, bf16[320,1,175]{...) while((s32[]{:T(128)}, f32[40,8,1,128]{3,2,1,0:T(1,128)S(1)}, ...), condition=%wide.region_1.2_spmd.clone, body=%wide.region_0.1_spmd.clone.sunk | while | flops 245767 | bytes 2293933 | solution.py:61
  159.4 1.6 dynamic_update_slice.25
  161.7 1.6 dynamic_update_slice.25
  164.0 1.6 dynamic_update_slice.25
  166.2 1.6 dynamic_update_slice.25
  168.5 1.6 dynamic_update_slice.25
  170.8 1.6 dynamic_update_slice.25
  173.1 1.6 dynamic_update_slice.25
  175.4 1.6 dynamic_update_slice.25
  177.6 1.6 dynamic_update_slice.25
  179.9 1.6 dynamic_update_slice.25
  182.2 1.6 dynamic_update_slice.25
  270.5 320.8 %all-reduce.4.cloned.1.call-done = f32[32,40,3,3,3]{1,0,4,3,2:T(8,128)} async-done(((f32[32,40,3,3,3]{1,0,4,3,2:T(8,128)}), f32[32,40,3,3,3]{1,0,4,3,2:T(8,128)}) %all-reduce.4.cloned.1.call-update) | async-done | bytes 138256 | tf_op jit(solution)/shard_map/psum | solution.py:103
  591.2 1.8 broadcast_multiply_fusion.1
  (644 shorter events, 159.1 us)
Async XLA Ops:
  7.2 134.3 %copy-start = (bf16[32,40,3,3,3]{1,0,4,3,2:T(8,128)(2,1)S(1)}, bf16[32,40,3,3,3]{1,0,4,3,2:T(8,128)(2,1)}, u32[]{:S(2)}) copy-start(bf16[32,40,3,3,3]{1,0,4,3,2:T(8,128)(2,1)} %param.11) | copy-start | bytes 207364
  7.2 584.1 %all-reduce.4.cloned.1.call-start = ((), (), s32[]{:S(2)}) async-start(), calls=%async_computation | async-start | bytes 884736 | tf_op jit(solution)/shard_map/psum | solution.py:103
  8.4 59.6 %collective-permute-start = (bf16[32,48,1,128]{3,0,1,2:T(8,128)(2,1)S(1)}, bf16[32,48,1,128]{3,0,1,2:T(8,128)(2,1)S(1)}, u32[]{:S(2)}, u32[]{:S(2)}) collective-permute-start(bf16[32,48,1,128]{3,0,1,2:T(8,128)(2,1)S(1)} %copy.82), channel_id=1, source_target_pairs={{0,16},{16,32},{32,48},{48,64},{64,80},{80,96},{96,112},{112,128},... | collective-permute-start | bytes 1179656 | tf_op jit(solution)/shard_map/ppermute | solution.py:21
  11.8 56.4 %collective-permute-start.1 = (bf16[32,48,1,128]{3,0,1,2:T(8,128)(2,1)S(1)}, bf16[32,48,1,128]{3,0,1,2:T(8,128)(2,1)S(1)}, u32[]{:S(2)}, u32[]{:S(2)}) collective-permute-start(bf16[32,48,1,128]{3,0,1,2:T(8,128)(2,1)S(1)} %copy.82), channel_id=1, source_target_pairs={{16,0},{32,16},{48,32},{64,48},{80,64},{96,80},{112,96},{128,112},... | collective-permute-start | bytes 1179656 | tf_op jit(solution)/shard_map/ppermute | solution.py:22
  17.5 2.4 collective-permute-start.4
  21.0 47.0 %copy-start.4 = (bf16[32,48,1,128]{3,1,2,0:T(8,128)(2,1)S(1)}, bf16[32,48,1,128]{3,1,2,0:T(8,128)(2,1)}, u32[]{:S(2)}) copy-start(bf16[32,48,1,128]{3,1,2,0:T(8,128)(2,1)} %param.10) | copy-start | bytes 1179652
  67.3 0.7 copy-start.2
  68.0 0.7 copy-start.7
  68.7 0.7 copy-start.9
  73.6 19.5 %collective-permute-start.2 = (bf16[32,48,3,1]{1,0,3,2:T(8,128)(2,1)S(1)}, bf16[32,48,3,1]{1,0,3,2:T(8,128)(2,1)S(1)}, u32[]{:S(2)}, u32[]{:S(2)}) collective-permute-start(bf16[32,48,3,1]{1,0,3,2:T(8,128)(2,1)S(1)} %copy.85), channel_id=1, source_target_pairs={{0,1},{1,2},{2,3},{3,4},{4,5},{5,6},{6,7},{7,8},{8,9},{9,10},{10,1... | collective-permute-start | bytes 27656 | tf_op jit(solution)/shard_map/ppermute | solution.py:21
  90.5 13.7 %collective-permute-start.3 = (bf16[32,48,3,1]{1,0,3,2:T(8,128)(2,1)S(1)}, bf16[32,48,3,1]{1,0,3,2:T(8,128)(2,1)S(1)}, u32[]{:S(2)}, u32[]{:S(2)}) collective-permute-start(bf16[32,48,3,1]{1,0,3,2:T(8,128)(2,1)S(1)} %copy.86), channel_id=1, source_target_pairs={{1,0},{2,1},{3,2},{4,3},{5,4},{6,5},{7,6},{8,7},{9,8},{10,9},{11,1... | collective-permute-start | bytes 27656 | tf_op jit(solution)/shard_map/ppermute | solution.py:22
  107.1 2.8 copy-start.1
  114.8 1.1 copy-start.10
  116.2 1.0 copy-start.5
  117.5 1.0 copy-start.8
  122.1 0.8 copy-start.6
  132.9 8.5 %copy-start.11 = (pred[8,17]{0,1:T(8,128)(4,1)S(1)}, pred[8,17]{0,1:T(8,128)(4,1)}, u32[]{:S(2)}) copy-start(pred[8,17]{0,1:T(8,128)(4,1)} %constant.149) | copy-start | bytes 412
  156.7 2.5 copy-start.3
  268.5 324.5 %collective-permute-start.5 = (f32[320,1,128]{2,0,1:T(8,128)S(1)}, f32[320,1,128]{2,0,1:T(8,128)S(1)}, u32[]{:S(2)}, u32[]{:S(2)}) collective-permute-start(f32[320,1,128]{2,0,1:T(8,128)S(1)} %pad.9), channel_id=1, source_target_pairs={{1,0},{2,1},{3,2},{4,3},{5,4},{6,5},{7,6},{8,7},{9,8},{10,9},{11,1... | collective-permute-start | bytes 491528 | tf_op jit(solution)/shard_map/ppermute | solution.py:11
Sparse Core Ops, SparseCore 0:
  123.0 468.2 all-reduce.3
where the time goes:
time: 602 us; the launch traced here: 601 us
  waiting for transfers between devices  330 us (55%)
  local copies, waits for them, and re-layouts  159 us (26%)
  other arithmetic  46 us (8%)
  starting transfers between devices  28.6 us (5%)
  matrix products  19.1 us (3%)
  between operations  14.3 us (2%)
    psum x1, waiting for transfers between devices, shards(): summed = lax.psum(kernel_local, ('rows', 'cols'))  321 us
    dynamic_update_slice x48, local copies, waits for them, and re-layouts, feature_one_level(): lax.dynamic_update_slice_in_dim(grad_ext, current + spread, offset, 2)  76.8 us
    dynamic_update_slice x48, local copies, waits for them, and re-layouts, correlate_one_level(): return lax.dynamic_update_slice_in_dim(volume, slab[:, None], level, 1)  29.6 us
    ppermute x2, starting transfers between devices, padded_2(): before = lax.ppermute(last, axis, up)  18.9 us
    add x48, other arithmetic, feature_one_level(): grad_left + slab * shifted.reshape(groups, group_size, band_rows, tile_wi...  16.9 us
    unnamed x29, local copies, waits for them, and re-layouts  12.7 us
  transfers between devices with their start and end apart: 7, of which 3 were waited for; matrix products, arithmetic and copies ran while one was open for 33% of the time, Pallas kernels for 0%

commit v1 on v0

--- a/solution.py
+++ b/solution.py
@@ -100,7 +100,7 @@
     flipped = jnp.transpose(jnp.flip(conv_weight, (2, 3, 4)), (1, 0, 2, 3, 4))
     layout = ("NCDHW", "OIDHW", "NCDHW")
     kernel_local = kernel_terms(volume, padded, levels, band_rows, tile_width)
-    summed = lax.psum(kernel_local, ("rows", "cols"))
+    summed = lax.psum(lax.psum(kernel_local, "cols"), "rows")
     grad_volume = lax.conv_general_dilated(
         padded[None],
         flipped,

time: 602 us -> 841 us (1.40)
  waiting for transfers between devices: 330 us -> 569 us
    psum x1 -> x2, waiting for transfers between devices: 321 us -> 560 us  [shards(): summed = lax.psum(lax.psum(kernel_local, 'cols'), 'rows')]
  transfers between devices with their start and end apart: 7 -> 8, of which waited for: 3 -> 4; matrix products, arithmetic and copies ran while one was open for 33% -> 23% of each run, Pallas kernels for 0% -> 0%
where the time goes in v1:
time: 841 us; the launch traced here: 840 us
  waiting for transfers between devices  569 us (68%)
  local copies, waits for them, and re-layouts  159 us (19%)
  other arithmetic  46 us (5%)
  starting transfers between devices  29 us (3%)
  matrix products  19.1 us (2%)
  between operations  14.3 us (2%)
    psum x2, waiting for transfers between devices, shards(): summed = lax.psum(lax.psum(kernel_local, 'cols'), 'rows')  560 us
    dynamic_update_slice x48, local copies, waits for them, and re-layouts, feature_one_level(): lax.dynamic_update_slice_in_dim(grad_ext, current + spread, offset, 2)  76.8 us
    dynamic_update_slice x48, local copies, waits for them, and re-layouts, correlate_one_level(): return lax.dynamic_update_slice_in_dim(volume, slab[:, None], level, 1)  29.6 us
    ppermute x2, starting transfers between devices, padded_2(): before = lax.ppermute(last, axis, up)  18.9 us
    add x48, other arithmetic, feature_one_level(): grad_left + slab * shifted.reshape(groups, group_size, band_rows, tile_wi...  16.9 us
  transfers between devices with their start and end apart: 8, of which 4 were waited for; matrix products, arithmetic and copies ran while one was open for 23% of the time, Pallas kernels for 0%

profile of v1, /device:TPU:2, one launch (start us, length us, event | category | flops | bytes accessed | tf_op | source)
XLA Modules:
  0.0 839.8 jit_solution(1299202233404010493)
XLA Ops:
  8.4 3.4 collective-permute-start
  11.8 5.7 collective-permute-start.1
  21.1 46.2 %while.33 = (s32[]{:T(128)}, f32[40,48,1,128]{3,2,1,0:T(1,128)}, bf16[320,1,175]{2,0,1:T(8,128)(2,1)S(1)}, f32[320,1,128]{2,1,0:T(1,128)S(1)}, s32[]{:T(128)}, /*index=5*/s32[]{:T(128)}, s32[]{:T(128)}, s32[]{:T(128)}) while((s32[]{:T(128)}, f32[40,48,1,128]{3,2,1,0:T(1,128)}, bf16[320,1,175]{2,0,1:T(8,128)(2,1)S(1)}, ...), condition=%wide.region_4.5_spmd, body=%wide.region_2.4_spmd.sunk | while | flops 122886 | bytes 840327 | solution.py:40
  69.5 1.6 fusion.78
  71.1 2.5 copy.85
  73.6 15.5 %collective-permute-start.2 = (bf16[32,48,3,1]{1,0,3,2:T(8,128)(2,1)S(1)}, bf16[32,48,3,1]{1,0,3,2:T(8,128)(2,1)S(1)}, u32[]{:S(2)}, u32[]{:S(2)}) collective-permute-start(bf16[32,48,3,1]{1,0,3,2:T(8,128)(2,1)S(1)} %copy.85), channel_id=1, source_target_pairs={{0,1},{1,2},{2,3},{3,4},{4,5},{5,6},{6,7},{7,8},{8,9},{9,10},{10,1... | collective-permute-start | bytes 27656 | tf_op jit(solution)/shard_map/ppermute | solution.py:21
  93.3 1.9 copy.87
  95.2 9.0 %collective-permute-done.3 = bf16[32,48,3,1]{1,0,3,2:T(8,128)(2,1)S(1)} collective-permute-done((bf16[32,48,3,1]{1,0,3,2:T(8,128)(2,1)S(1)}, bf16[32,48,3,1]{1,0,3,2:T(8,128)(2,1)S(1)}, u32[]{:S(2)}, u32[]{:S(2)}) %collective-permute-start.3) | collective-permute-done | bytes 9248 | tf_op jit(solution)/shard_map/ppermute | solution.py:22
  104.2 2.9 copy.88
  107.1 2.7 fusion.16
  109.8 2.7 fusion.80
  123.1 5.7 copy.134
  128.9 4.3 pad.10.clone
  133.2 7.2 copy.91
  141.7 10.0 %fusion.17 = f32[48,1,8,17,40]{4,2,3,1,0:T(8,128)} fusion(bf16[32,40,3,3,3]{1,0,4,3,2:T(8,128)(2,1)S(1)} %copy-done, bf16[32,50,3,1,7,2]{0,4,5,2,1,3:T(8,128)(2,1)S(1)} %slice.141, bf16[32,50,3,1,8,17]{0,4,5,2,1,3:T(8,128)(2,1)} %copy.91, pred[8,17]{0,1:T(8,128)(4,1)S(1)} %copy-done.11), kind=kOutput, calls=%fused_computation.30 | convolution fusion | flops 455854080 | bytes 2553736 | tf_op jit(solution)/shard_map/conv_general_dilated | solution.py:104
  151.7 3.5 copy.92
  155.3 1.7 slice_bitcast_fusion
  156.9 2.5 copy.94
  159.5 109.2 %while.34 = (s32[]{:T(128)}, f32[40,8,1,128]{3,2,1,0:T(1,128)S(1)}, f32[320,1,175]{2,0,1:T(8,128)S(1)}, f32[40,48,1,128]{3,0,2,1:T(8,128)S(1)}, bf16[320,1,175]{...) while((s32[]{:T(128)}, f32[40,8,1,128]{3,2,1,0:T(1,128)S(1)}, ...), condition=%wide.region_1.2_spmd.clone, body=%wide.region_0.1_spmd.clone.sunk | while | flops 245767 | bytes 2293933 | solution.py:61
  159.7 1.6 dynamic_update_slice.25
  161.9 1.6 dynamic_update_slice.25
  164.2 1.6 dynamic_update_slice.25
  166.5 1.6 dynamic_update_slice.25
  168.8 1.6 dynamic_update_slice.25
  171.1 1.6 dynamic_update_slice.25
  173.3 1.6 dynamic_update_slice.25
  175.6 1.6 dynamic_update_slice.25
  177.9 1.6 dynamic_update_slice.25
  180.2 1.6 dynamic_update_slice.25
  270.7 114.4 %all-reduce.5.cloned.1.call-done = f32[32,40,3,3,3]{1,0,4,3,2:T(8,128)} async-done(((f32[32,40,3,3,3]{1,0,4,3,2:T(8,128)}), f32[32,40,3,3,3]{1,0,4,3,2:T(8,128)}) %all-reduce.5.cloned.1.call-update) | async-done | bytes 138256 | tf_op jit(solution)/shard_map/psum | solution.py:103
  385.9 445.2 %all-reduce.7.cloned.1.call-done = f32[32,40,3,3,3]{1,0,4,3,2:T(8,128)} async-done(((f32[32,40,3,3,3]{1,0,4,3,2:T(8,128)}), f32[32,40,3,3,3]{1,0,4,3,2:T(8,128)}) %all-reduce.7.cloned.1.call-update) | async-done | bytes 138256 | tf_op jit(solution)/shard_map/psum | solution.py:103
  831.1 1.8 broadcast_multiply_fusion.1
  (647 shorter events, 161.1 us)
Async XLA Ops:
  7.2 134.5 %copy-start = (bf16[32,40,3,3,3]{1,0,4,3,2:T(8,128)(2,1)S(1)}, bf16[32,40,3,3,3]{1,0,4,3,2:T(8,128)(2,1)}, u32[]{:S(2)}) copy-start(bf16[32,40,3,3,3]{1,0,4,3,2:T(8,128)(2,1)} %param.11) | copy-start | bytes 207364
  7.2 377.9 %all-reduce.5.cloned.1.call-start = ((), (), s32[]{:S(2)}) async-start(), calls=%async_computation | async-start | bytes 884736 | tf_op jit(solution)/shard_map/psum | solution.py:103
  8.4 59.6 %collective-permute-start = (bf16[32,48,1,128]{3,0,1,2:T(8,128)(2,1)S(1)}, bf16[32,48,1,128]{3,0,1,2:T(8,128)(2,1)S(1)}, u32[]{:S(2)}, u32[]{:S(2)}) collective-permute-start(bf16[32,48,1,128]{3,0,1,2:T(8,128)(2,1)S(1)} %copy.82), channel_id=1, source_target_pairs={{0,16},{16,32},{32,48},{48,64},{64,80},{80,96},{96,112},{112,128},... | collective-permute-start | bytes 1179656 | tf_op jit(solution)/shard_map/ppermute | solution.py:21
  11.8 56.4 %collective-permute-start.1 = (bf16[32,48,1,128]{3,0,1,2:T(8,128)(2,1)S(1)}, bf16[32,48,1,128]{3,0,1,2:T(8,128)(2,1)S(1)}, u32[]{:S(2)}, u32[]{:S(2)}) collective-permute-start(bf16[32,48,1,128]{3,0,1,2:T(8,128)(2,1)S(1)} %copy.82), channel_id=1, source_target_pairs={{16,0},{32,16},{48,32},{64,48},{80,64},{96,80},{112,96},{128,112},... | collective-permute-start | bytes 1179656 | tf_op jit(solution)/shard_map/ppermute | solution.py:22
  17.5 2.4 collective-permute-start.4
  21.0 47.0 %copy-start.4 = (bf16[32,48,1,128]{3,1,2,0:T(8,128)(2,1)S(1)}, bf16[32,48,1,128]{3,1,2,0:T(8,128)(2,1)}, u32[]{:S(2)}) copy-start(bf16[32,48,1,128]{3,1,2,0:T(8,128)(2,1)} %param.10) | copy-start | bytes 1179652
  67.3 0.7 copy-start.2
  68.0 0.7 copy-start.7
  68.7 0.7 copy-start.9
  73.6 19.6 %collective-permute-start.2 = (bf16[32,48,3,1]{1,0,3,2:T(8,128)(2,1)S(1)}, bf16[32,48,3,1]{1,0,3,2:T(8,128)(2,1)S(1)}, u32[]{:S(2)}, u32[]{:S(2)}) collective-permute-start(bf16[32,48,3,1]{1,0,3,2:T(8,128)(2,1)S(1)} %copy.85), channel_id=1, source_target_pairs={{0,1},{1,2},{2,3},{3,4},{4,5},{5,6},{6,7},{7,8},{8,9},{9,10},{10,1... | collective-permute-start | bytes 27656 | tf_op jit(solution)/shard_map/ppermute | solution.py:21
  90.5 13.7 %collective-permute-start.3 = (bf16[32,48,3,1]{1,0,3,2:T(8,128)(2,1)S(1)}, bf16[32,48,3,1]{1,0,3,2:T(8,128)(2,1)S(1)}, u32[]{:S(2)}, u32[]{:S(2)}) collective-permute-start(bf16[32,48,3,1]{1,0,3,2:T(8,128)(2,1)S(1)} %copy.86), channel_id=1, source_target_pairs={{1,0},{2,1},{3,2},{4,3},{5,4},{6,5},{7,6},{8,7},{9,8},{10,9},{11,1... | collective-permute-start | bytes 27656 | tf_op jit(solution)/shard_map/ppermute | solution.py:22
  107.1 2.8 copy-start.1
  114.8 1.1 copy-start.10
  116.2 1.0 copy-start.5
  117.5 1.0 copy-start.8
  122.1 0.8 copy-start.6
  122.9 708.3 %all-reduce.7.cloned.1.call-start = ((), (), s32[]{:S(2)}) async-start(), calls=%async_computation.1 | async-start | bytes 884736 | tf_op jit(solution)/shard_map/psum | solution.py:103
  133.2 8.5 %copy-start.11 = (pred[8,17]{0,1:T(8,128)(4,1)S(1)}, pred[8,17]{0,1:T(8,128)(4,1)}, u32[]{:S(2)}) copy-start(pred[8,17]{0,1:T(8,128)(4,1)} %constant.149) | copy-start | bytes 412
  156.9 2.5 copy-start.3
  268.8 116.4 %collective-permute-start.5 = (f32[320,1,128]{2,0,1:T(8,128)S(1)}, f32[320,1,128]{2,0,1:T(8,128)S(1)}, u32[]{:S(2)}, u32[]{:S(2)}) collective-permute-start(f32[320,1,128]{2,0,1:T(8,128)S(1)} %pad.9), channel_id=1, source_target_pairs={{1,0},{2,1},{3,2},{4,3},{5,4},{6,5},{7,6},{8,7},{9,8},{10,9},{11,1... | collective-permute-start | bytes 491528 | tf_op jit(solution)/shard_map/ppermute | solution.py:11
Sparse Core Ops, SparseCore 0:
  123.0 262.0 all-reduce.4
  388.3 442.7 all-reduce.6
